TPU v7x, 512 devices: a whole 4x8x8 slice. The times are simulated.
512 devices in a mesh: band: 8 (over y_lo, x), dom: 64 (over z, y_hi, core).
Axes of the slice: x: 4, y: 8 (y_hi: 4, y_lo: 2; y = y_hi * 2 + y_lo), z: 8, core: 2. Of those that a mesh axis runs over, the one named last changes fastest.
Arguments:
- orbitals: float32 [256, 384, 256], P('band', 'dom'), may hold values from -6 to 6
- potential: float32 [384, 256], P('dom'), may hold values from -1 to 0.5
Outputs:
- orthonormal: float32 [256, 384, 256], P('band', 'dom')
All inputs are finite; a program needn't handle non-finite values.
Results may differ from a plain program's by a relative error of at most 0.00007.
Values sent between devices are 32-bit elements; how exact they have to be, the bound alone decides.
A program may use at most 64 MiB of HBM per device.

v0:
```python
import jax
import jax.numpy as jnp
from jax import lax
from jax.sharding import PartitionSpec as P

NX = 16


weights = (
    -5369.0 / 1800.0,
    12.0 / 7.0,
    -15.0 / 56.0,
    10.0 / 189.0,
    -1.0 / 112.0,
    2.0 / 1925.0,
    -1.0 / 16632.0,
)
centre = 6.0
half_width = 5.0


def with_halo(cells, sides, width):
    for axis, dim in sides:
        count = lax.axis_size(axis)
        head = lax.slice_in_dim(cells, 0, width, axis=dim)
        tail = lax.slice_in_dim(cells, cells.shape[dim] - width, cells.shape[dim], axis=dim)
        cells = jnp.concatenate(
            [
                lax.ppermute(tail, axis, [(i, (i + 1) % count) for i in range(count)]),
                cells,
                lax.ppermute(head, axis, [((i + 1) % count, i) for i in range(count)]),
            ],
            axis=dim,
        )
    return cells


def hamiltonian(field, potential):
    bands, planes, width = field.shape
    padded = with_halo(field, (("dom", 1),), 6)
    lap = 3.0 * weights[0] * field
    for step in range(1, 7):
        lap = lap + weights[step] * (
            padded[:, 6 - step : 6 - step + planes] + padded[:, 6 + step : 6 + step + planes]
        )
    column = lax.broadcasted_iota(jnp.int32, (1, 1, width), 2) % NX
    for step in range(1, 7):
        along_y = jnp.roll(field, step * NX, 2) + jnp.roll(field, -step * NX, 2)
        lower = jnp.where(column >= step, jnp.roll(field, step, 2), jnp.roll(field, step - NX, 2))
        upper = jnp.where(
            column < NX - step, jnp.roll(field, -step, 2), jnp.roll(field, NX - step, 2)
        )
        lap = lap + weights[step] * (along_y + lower + upper)
    return -0.5 * lap + potential[None] * field


def scaled(field, potential):
    return (hamiltonian(field, potential) - centre * field) / half_width


def inverse_factor(margin):
    factor = jnp.linalg.cholesky(margin)
    return lax.linalg.triangular_solve(
        factor, jnp.eye(margin.shape[0], dtype=margin.dtype), left_side=True, lower=True
    )


def on_device(orbitals, potential):
    first = scaled(orbitals, potential)
    second = 2.0 * scaled(first, potential) - orbitals
    filtered = 2.0 * scaled(second, potential) - first
    orb_local, planes, width = filtered.shape
    groups = lax.axis_size("band")
    total_bands = orb_local * groups
    cells = jnp.float32(lax.axis_size("dom") * planes * width)
    whole = lax.all_gather(filtered, "band", axis=0, tiled=True)
    whole_flat = whole.reshape(total_bands, planes * width)
    mine_flat = filtered.reshape(orb_local, planes * width)
    rows = jnp.dot(
        mine_flat, whole_flat.T, precision=lax.Precision.HIGHEST, preferred_element_type=jnp.float32
    )
    summed = lax.psum(rows, "dom")
    margin = lax.all_gather(summed, "band", axis=0, tiled=True) / cells
    inverse = inverse_factor(margin)
    my_rows = lax.dynamic_slice_in_dim(inverse, lax.axis_index("band") * orb_local, orb_local, 0)
    result = jnp.dot(
        my_rows, whole_flat, precision=lax.Precision.HIGHEST, preferred_element_type=jnp.float32
    )
    return result.reshape(orb_local, planes, width)


def solution(mesh):
    placed = (P("band", "dom", None), P("dom", None))
    return jax.shard_map(
        on_device, mesh=mesh, in_specs=placed, out_specs=P("band", "dom", None), check_vma=False
    )
```

profile of v0, /device:TPU:8, one launch (start us, length us, event | category | flops | bytes accessed | tf_op | source)
XLA Modules:
  0.0 491.9 jit_solution(13760203766258567575)
XLA Ops:
  6.5 2.0 collective-permute-start
  8.6 13.2 %collective-permute-start.1 = (f32[32,6,256]{2,0,1:T(8,128)}, f32[32,6,256]{2,0,1:T(8,128)S(1)}, u32[]{:S(2)}, u32[]{:S(2)}) collective-permute-start(f32[32,6,256]{2,0,1:T(8,128)} %param.2), channel_id=1, source_target_pairs={{1,0},{2,1},{3,2},{4,3},{5,4},{6,5},{7,6},{8,7},{9,8},{10,9},{11,1... | collective-permute-start | bytes 589832 | tf_op jit(solution)/shard_map/ppermute | solution.py:31
  21.9 1.1 fusion.230
  23.0 1.1 fusion.232
  27.9 2.0 broadcast_multiply_fusion.1
  33.7 1.9 collective-permute-start.2
  35.6 7.9 %collective-permute-start.3 = (f32[32,6,256]{2,0,1:T(8,128)S(1)}, f32[32,6,256]{2,0,1:T(8,128)S(1)}, u32[]{:S(2)}, u32[]{:S(2)}) collective-permute-start(f32[32,6,256]{2,0,1:T(8,128)S(1)} %get-tuple-element.21), channel_id=1, source_target_pairs={{1,0},{2,1},{3,2},{4,3},{5,4},{6,5},{7,6},{8,7},{9,8},{10,9},{11,1... | collective-permute-start | bytes 589832 | tf_op jit(solution)/shard_map/ppermute | solution.py:31
  43.6 2.9 collective-permute-done.2
  46.7 2.4 multiply_subtract_fusion.1
  51.2 1.9 collective-permute-start.4
  53.2 8.3 %collective-permute-start.5 = (f32[32,6,256]{2,0,1:T(8,128)S(1)}, f32[32,6,256]{2,0,1:T(8,128)S(1)}, u32[]{:S(2)}, u32[]{:S(2)}) collective-permute-start(f32[32,6,256]{2,0,1:T(8,128)S(1)} %multiply_subtract_fusion.1), channel_id=1, source_target_pairs={{1,0},{2,1},{3,2},{4,3},{5,4},{6,5},{7,6},{8,7},{9,8},{10,9},{11,1... | collective-permute-start | bytes 589832 | tf_op jit(solution)/shard_map/ppermute | solution.py:31
  63.2 1.3 collective-permute-done.5
  64.4 3.0 multiply_subtract_fusion
  67.6 45.6 %all-gather.2.cloned.1.call-done = f32[256,6,256]{2,0,1:T(8,128)} async-done(((f32[32,6,256]{2,0,1:T(8,128)}), f32[256,6,256]{2,0,1:T(8,128)}) %all-gather.2.cloned.1.call-update) | async-done | bytes 1572880 | tf_op jit(solution)/shard_map/all_gather | solution.py:76
  113.1 3.0 convolution_bitcast_fusion
  116.2 276.5 %psum.7 = f32[32,256]{1,0:T(8,128)S(1)} all-reduce(f32[32,256]{1,0:T(8,128)S(1)} %convolution_bitcast_fusion), channel_id=1, replica_groups=mesh['band'=8,'dom'=64] {'dom'}, use_global_device_ids=true, to_apply=%region_0.1 | all-reduce | flops 8192 | bytes 65536 | tf_op jit(solution)/shard_map/psum | solution.py:82
  392.6 28.4 %all_gather.7 = f32[256,256]{1,0:T(8,128)S(1)} all-gather(f32[32,256]{1,0:T(8,128)S(1)} %psum.7), channel_id=1, replica_groups=mesh['band'=8,'dom'=64] {'band'}, dimensions={0}, use_global_device_ids=true | all-gather | bytes 294912 | tf_op jit(solution)/shard_map/all_gather | solution.py:83
  421.4 11.7 %cholesky.50 = f32[128,128]{1,0:T(8,128)S(1)} custom-call(f32[128,128]{1,0:T(8,128)S(1)} %cholesky.118), custom_call_target="Cholesky" | custom-call | tf_op jit(solution)/shard_map/jit(cholesky)/cholesky | solution.py:62
  433.2 9.8 %custom-call.14 = f32[1,128,128]{1,2,0:T(8,128)S(1)} custom-call(f32[1,128,128]{2,1,0:T(8,128)S(1)} %get-tuple-element.246), custom_call_target="InvertDiagBlocksLowerTriangular" | custom-call | tf_op jit(solution)/shard_map/jit(cholesky)/cholesky | solution.py:62
  443.2 0.3 convolution_subtract_fusion.1
  443.5 11.7 %cholesky.105 = f32[128,128]{1,0:T(8,128)S(1)} custom-call(f32[128,128]{1,0:T(8,128)S(1)} %convolution_subtract_fusion.1), custom_call_target="Cholesky" | custom-call | tf_op jit(solution)/shard_map/jit(cholesky)/cholesky | solution.py:62
  455.2 0.6 compare_reduce_fusion
  455.8 0.6 compare_reduce_fusion.1
  457.8 4.0 while.1
  458.0 0.6 fusion.272
  458.6 1.3 bitcast_dynamic-update-slice_fusion.2
  459.9 0.6 fusion.272
  460.5 1.3 bitcast_dynamic-update-slice_fusion.2
  461.8 19.7 %custom-call.15 = f32[2,128,128]{1,2,0:T(8,128)S(1)} custom-call(f32[2,128,128]{2,1,0:T(8,128)S(1)} %get-tuple-element.12), custom_call_target="InvertDiagBlocksLowerTriangular" | custom-call | tf_op jit(solution)/shard_map/triangular_solve | solution.py:63
  482.0 0.3 fusion.146
  482.4 0.5 copy.10
  482.8 2.2 fusion
  (146 shorter events, 12.2 us)
Async XLA Ops:
  6.5 17.6 %copy-start = (f32[32,6,256]{2,0,1:T(8,128)S(1)}, f32[32,6,256]{2,0,1:T(8,128)}, u32[]{:S(2)}) copy-start(f32[32,6,256]{2,0,1:T(8,128)} %param.2) | copy-start | bytes 589828
  6.5 106.6 %all-gather.2.cloned.1.call-start = ((), (), s32[]{:S(2)}) async-start(), calls=%async_computation | async-start | bytes 1769472 | tf_op jit(solution)/shard_map/all_gather | solution.py:76
  6.5 21.3 %collective-permute-start = (f32[32,6,256]{2,0,1:T(8,128)}, f32[32,6,256]{2,0,1:T(8,128)S(1)}, u32[]{:S(2)}, u32[]{:S(2)}) collective-permute-start(f32[32,6,256]{2,0,1:T(8,128)} %param.2), channel_id=1, source_target_pairs={{0,1},{1,2},{2,3},{3,4},{4,5},{5,6},{6,7},{7,8},{8,9},{9,10},{10,1... | collective-permute-start | bytes 589832 | tf_op jit(solution)/shard_map/ppermute | solution.py:29
  8.6 19.3 %collective-permute-start.1 = (f32[32,6,256]{2,0,1:T(8,128)}, f32[32,6,256]{2,0,1:T(8,128)S(1)}, u32[]{:S(2)}, u32[]{:S(2)}) collective-permute-start(f32[32,6,256]{2,0,1:T(8,128)} %param.2), channel_id=1, source_target_pairs={{1,0},{2,1},{3,2},{4,3},{5,4},{6,5},{7,6},{8,7},{9,8},{10,9},{11,1... | collective-permute-start | bytes 589832 | tf_op jit(solution)/shard_map/ppermute | solution.py:31
  27.0 0.8 copy-start.2
  33.7 12.8 %collective-permute-start.2 = (f32[32,6,256]{2,0,1:T(8,128)S(1)}, f32[32,6,256]{2,0,1:T(8,128)S(1)}, u32[]{:S(2)}, u32[]{:S(2)}) collective-permute-start(f32[32,6,256]{2,0,1:T(8,128)S(1)} %get-tuple-element.21), channel_id=1, source_target_pairs={{0,1},{1,2},{2,3},{3,4},{4,5},{5,6},{6,7},{7,8},{8,9},{9,10},{10,1... | collective-permute-start | bytes 589832 | tf_op jit(solution)/shard_map/ppermute | solution.py:29
  35.6 11.1 %collective-permute-start.3 = (f32[32,6,256]{2,0,1:T(8,128)S(1)}, f32[32,6,256]{2,0,1:T(8,128)S(1)}, u32[]{:S(2)}, u32[]{:S(2)}) collective-permute-start(f32[32,6,256]{2,0,1:T(8,128)S(1)} %get-tuple-element.21), channel_id=1, source_target_pairs={{1,0},{2,1},{3,2},{4,3},{5,4},{6,5},{7,6},{8,7},{9,8},{10,9},{11,1... | collective-permute-start | bytes 589832 | tf_op jit(solution)/shard_map/ppermute | solution.py:31
  51.2 11.9 %collective-permute-start.4 = (f32[32,6,256]{2,0,1:T(8,128)S(1)}, f32[32,6,256]{2,0,1:T(8,128)S(1)}, u32[]{:S(2)}, u32[]{:S(2)}) collective-permute-start(f32[32,6,256]{2,0,1:T(8,128)S(1)} %multiply_subtract_fusion.1), channel_id=1, source_target_pairs={{0,1},{1,2},{2,3},{3,4},{4,5},{5,6},{6,7},{7,8},{8,9},{9,10},{10,1... | collective-permute-start | bytes 589832 | tf_op jit(solution)/shard_map/ppermute | solution.py:29
  53.2 11.3 %collective-permute-start.5 = (f32[32,6,256]{2,0,1:T(8,128)S(1)}, f32[32,6,256]{2,0,1:T(8,128)S(1)}, u32[]{:S(2)}, u32[]{:S(2)}) collective-permute-start(f32[32,6,256]{2,0,1:T(8,128)S(1)} %multiply_subtract_fusion.1), channel_id=1, source_target_pairs={{1,0},{2,1},{3,2},{4,3},{5,4},{6,5},{7,6},{8,7},{9,8},{10,9},{11,1... | collective-permute-start | bytes 589832 | tf_op jit(solution)/shard_map/ppermute | solution.py:31
  433.1 49.2 %copy-start.1 = (f32[256,6,256]{2,0,1:T(8,128)S(1)}, f32[256,6,256]{2,0,1:T(8,128)}, u32[]{:S(2)}) copy-start(f32[256,6,256]{2,0,1:T(8,128)} %all-gather.2.cloned.1.call-done) | copy-start | bytes 4718596
Sparse Core Ops, SparseCore 0:
  67.6 45.4 all-gather.1
where the time goes:
time: 492 us
  blocking collectives  305 us (62%)
  other arithmetic  61.8 us (13%)
  waiting for transfers between devices  50 us (10%)
  starting transfers between devices  35.2 us (7%)
  local copies, waits for them, and re-layouts  17.5 us (4%)
  between operations  15.8 us (3%)
  matrix products  6.53 us (1%)
    psum x1, blocking collectives, on_device(): summed = lax.psum(rows, 'dom')  276 us
    all_gather x1, waiting for transfers between devices, on_device(): whole = lax.all_gather(filtered, 'band', axis=0, tiled=True)  45.6 us
    another operation x7, other arithmetic, inverse_factor(): factor = jnp.linalg.cholesky(margin)  34.6 us
    ppermute x3, starting transfers between devices, with_halo(): lax.ppermute(head, axis, [((i + 1) % count, i) for i in range(count)])  29.3 us
    all_gather x1, blocking collectives, on_device(): margin = lax.all_gather(summed, 'band', axis=0, tiled=True) / cells  28.4 us
    another operation x3, other arithmetic, inverse_factor(): lax.linalg.triangular_solve(factor, jnp.eye(margin.shape[0], dtype=margin...  19.7 us
  transfers between devices with their start and end apart: 7, of which 4 were waited for; matrix products, arithmetic and copies ran while one was open for 2% of the time, Pallas kernels for 0%

commit v1 on v0

v1 whole, which is shorter than its diff:
```python
import jax
import jax.numpy as jnp
import numpy as np
from jax import lax
from jax.experimental import pallas as pl
from jax.experimental.pallas import tpu as pltpu
from jax.sharding import PartitionSpec as P

NX = 16
ORB = 32
BANDS = 256
PLANES = 6
WIDTH = 256
CELLS = 98304
GROUPS = 8
CHUNKS = 4
CORB = ORB // CHUNKS
PIVOTS = 4
HALF = BANDS // 2

weights = (
    -5369.0 / 1800.0,
    12.0 / 7.0,
    -15.0 / 56.0,
    10.0 / 189.0,
    -1.0 / 112.0,
    2.0 / 1925.0,
    -1.0 / 16632.0,
)
centre = 6.0
half_width = 5.0
along_z = [-0.5 * w / half_width for w in weights]

FAR_BAND = (2, 6, 3, 5, 1, 7, 4)
FAR_HI = (2, 1, 3)
FAR_Z = (4, 3, 5, 2, 6, 1, 7)
MESH = pl.DeviceIdType.MESH
EXACT = lax.Precision.HIGHEST
F32 = jnp.float32


def plane_matrix():
    out = np.zeros((WIDTH, WIDTH))
    for cell in range(WIDTH):
        y, x = divmod(cell, NX)
        out[cell, cell] += 3.0 * weights[0]
        for step in range(1, 7):
            for sign in (-1, 1):
                out[(y + sign * step) % NX * NX + x, cell] += weights[step]
                out[y * NX + (x + sign * step) % NX, cell] += weights[step]
    return (-0.5 / half_width * out).astype(np.float32)


def product(a, b, dims=((1,), (0,))):
    return lax.dot_general(
        a, b, (dims, ((), ())), precision=EXACT, preferred_element_type=F32
    )


def greet(partners):
    barrier = pltpu.get_barrier_semaphore()
    for partner in partners:
        pl.semaphore_signal(barrier, inc=1, device_id=partner, device_id_type=MESH)
    pl.semaphore_wait(barrier, len(partners))


def send(src, dst, send_sem, recv_sem, device):
    copy = pltpu.make_async_remote_copy(
        src_ref=src,
        dst_ref=dst,
        send_sem=send_sem,
        recv_sem=recv_sem,
        device_id=device,
        device_id_type=MESH,
    )
    return copy


def eliminate(groups, size):
    lane = lax.broadcasted_iota(jnp.int32, (8, size), 1)
    sublane = lax.broadcasted_iota(jnp.int32, (8, size), 0)
    groups = list(groups)
    span = range(PIVOTS)

    def spread_lane(tile, at):
        return jnp.broadcast_to(tile[:, at:at + 1], (8, size))

    def spread_row(tile, at):
        return jnp.broadcast_to(tile[at:at + 1, :], (8, size))

    entry = None
    for first in range(0, size, PIVOTS):
        home, off = divmod(first, 8)
        live = range(home, size // 8)
        columns = [{g: spread_lane(groups[g], first + q) for g in live} for q in span]
        if entry is None:
            entry = [[spread_row(columns[q][home], off + p) for q in range(p + 1)] for p in span]
        following = first + PIVOTS
        if following < size:
            near, near_off = divmod(following, 8)
            ahead = [spread_lane(groups[near], following + q) for q in span]
            ahead = [[spread_row(ahead[q], near_off + p) for q in range(p + 1)] for p in span]
            coupling = [[spread_row(columns[t][near], near_off + p) for t in span] for p in span]
        inside = (lane >= first) & (lane < following)
        scales = []
        low = [[None] * PIVOTS for _ in span]
        for q in span:
            value = entry[q][q]
            for t in range(q):
                value = value - low[q][t] * low[q][t]
            scales.append(lax.rsqrt(value))
            for p in range(q + 1, PIVOTS):
                value = entry[p][q]
                for t in range(q):
                    value = value - low[p][t] * low[q][t]
                low[p][q] = value * scales[q]
        if following < size:
            for t in span:
                for p in span:
                    value = coupling[p][t]
                    for u in range(t):
                        value = value - low[t][u] * coupling[p][u]
                    coupling[p][t] = value * scales[t]
            for p in span:
                for q in range(p + 1):
                    value = ahead[p][q]
                    for t in span:
                        value = value - coupling[p][t] * coupling[q][t]
                    ahead[p][q] = value
            entry = ahead
        scaled = []
        pivot_rows = []
        for q in span:
            column = dict(columns[q])
            row = spread_row(groups[home], off + q)
            row = jnp.where(inside, jnp.where(lane == first + q, 1.0, 0.0), row)
            for t in range(q):
                row = row - low[q][t] * pivot_rows[t]
                for g in live:
                    column[g] = column[g] - low[q][t] * scaled[t][g]
            pivot_rows.append(row * scales[q])
            scaled.append({g: column[g] * scales[q] for g in live})
        for g in live:
            if g == home and following % 8 == 0:
                new = groups[g]
            else:
                new = jnp.where(inside, 0.0, groups[g])
                for q in span:
                    new = new - scaled[q][g] * pivot_rows[q]
                if g == home:
                    new = jnp.where(sublane < off, groups[g], new)
            if g == home:
                for q in span:
                    new = jnp.where(sublane == off + q, pivot_rows[q], new)
            groups[g] = new
    return groups


def rows_of(b):
    return pl.ds(pl.multiple_of(b * ORB, ORB), ORB)


def whole_kernel(x_ref, pot_hbm, mat_hbm, out_ref, pot_ref, mat_ref, cells_ref, margin_ref, made, work,
                 field, local, part, band_in, hi_in, z_in,
                 halo_send, halo_recv, cell_sems, load_sems, sems, row_sems):
    band = lax.axis_index("band")
    dom = lax.axis_index("dom")
    count = lax.axis_size("dom")
    core = lax.rem(dom, 2)
    hi = lax.rem(lax.div(dom, 2), 4)
    z = lax.div(dom, 8)
    left = (band, lax.rem(dom + count - 1, count))
    right = (band, lax.rem(dom + 1, count))
    bands = [lax.rem(band + k, 8) for k in range(8)]
    senders = [lax.rem(band + 8 - k, 8) for k in range(8)]
    to_band = [(bands[k], dom) for k in range(8)]
    to_hi = [(band, z * 8 + lax.rem(hi + k, 4) * 2 + core) for k in range(4)]
    to_z = [(band, lax.rem(z + k, 8) * 8 + hi * 2 + core) for k in range(8)]
    has_plane = band < PLANES
    loads = [
        pltpu.make_async_copy(x_ref, field.at[0, pl.ds(PLANES, PLANES)], load_sems.at[0]),
        pltpu.make_async_copy(mat_hbm, mat_ref, load_sems.at[1]),
        pltpu.make_async_copy(pot_hbm, pot_ref, load_sems.at[2]),
    ]
    for load in loads:
        load.start()
    to_sixteen = [
        (k, flip, (bands[k], dom + flip * (1 - 2 * core)))
        for k in FAR_BAND + (0,) for flip in range(2) if k + flip > 0
    ]
    own = core * 8 + band
    greet([left, right] + [where for _, _, where in to_sixteen] + to_hi[1:] + to_z[1:])

    def chunk(c):
        return pl.ds(c * CORB, CORB)

    def halo(r, c):
        if r == 0:
            own = x_ref.at[:, chunk(c)]
        else:
            own = field.at[r, pl.ds(PLANES, PLANES), chunk(c)]
        return (
            send(own, field.at[r, pl.ds(2 * PLANES, PLANES), chunk(c)],
                 halo_send.at[r, c, 0], halo_recv.at[r, c, 0], left),
            send(own, field.at[r, pl.ds(0, PLANES), chunk(c)],
                 halo_send.at[r, c, 1], halo_recv.at[r, c, 1], right),
        )

    def in_plane(r, c):
        own = field[r, PLANES:2 * PLANES, c * CORB:(c + 1) * CORB, :]
        flat = own.reshape(PLANES * CORB, WIDTH)
        side = product(flat, mat_ref[...]).reshape(PLANES, CORB, WIDTH)
        for p in range(PLANES):
            diag = (pot_ref[p:p + 1, :] - centre) * (1.0 / half_width)
            local[c, p] = side[p] + diag * own[p]

    def rows_in(c):
        return pl.ds(pl.multiple_of(band * ORB, ORB) + c * CORB, CORB)

    def to_plane(k, c):
        return send(field.at[3, PLANES + bands[k], chunk(c)], cells_ref.at[rows_in(c)],
                    cell_sems.at[0], cell_sems.at[1], to_band[k])

    def all_planes():
        others = cells_ref.at[pl.ds(0, BANDS - ORB)]
        return send(others, others, cell_sems.at[0], cell_sems.at[1], to_band[1])

    for c in range(CHUNKS):
        for copy in halo(0, c):
            copy.start()
    for load in loads:
        load.wait()
    for c in range(CHUNKS):
        in_plane(0, c)
    for r in range(3):
        for c in range(CHUNKS):
            rows = slice(c * CORB, (c + 1) * CORB)
            for copy in halo(r, c):
                copy.wait_recv()
            for p in range(PLANES):
                total = local[c, p]
                for step in range(1, 7):
                    total = total + along_z[step] * (
                        field[r, PLANES + p - step, rows, :] + field[r, PLANES + p + step, rows, :]
                    )
                if r > 0:
                    total = 2.0 * total - field[r - 1, PLANES + p, rows, :]
                field[r + 1, PLANES + p, rows, :] = total
            if r < 2:
                for copy in halo(r + 1, c):
                    copy.start()
                in_plane(r + 1, c)
            else:
                for k in FAR_BAND:
                    @pl.when(bands[k] < PLANES)
                    def _():
                        to_plane(k, c).start()

                @pl.when(has_plane)
                def _():
                    cells_ref[rows_in(c), :] = field[3, PLANES + band, rows, :]

    def sixteenth(k, flip):
        return (core + flip * (1 - 2 * core)) * 8 + bands[k]

    parts = (pl.ds(0, 8), pl.ds(8, 16))

    def total_of(ref, count, i):
        total = ref[0, parts[i], :]
        for t in range(1, count):
            total = total + ref[t, parts[i], :]
        return total

    def bytes_of(ref, count, stage, i):
        some = ref.at[pl.ds(0, count), parts[i]]
        return send(some, some, sems.at[stage, 0, i], sems.at[stage, 1, i], left)

    def to_owner(k, flip, where, i):
        return send(part.at[sixteenth(k, flip), parts[i]], band_in.at[core * PLANES + band, parts[i]],
                    sems.at[0, 0, i], sems.at[0, 1, i], where)

    @pl.when(has_plane)
    def _():
        all_planes().wait_recv()
        for i in range(2):
            if i == 0:
                blocks = (product(cells_ref[:HALF, :], cells_ref[:HALF, :], ((1,), (1,))),)
            else:
                both = product(cells_ref[HALF:, :], cells_ref[...], ((1,), (1,)))
                blocks = (both[:, :HALF], both[:, HALF:])
            for q in range(16):
                for n, piece in enumerate(blocks):
                    part[q, 8 * (i + n):8 * (i + n) + 8, :] = piece[8 * q:8 * q + 8, :]
            for target in to_sixteen:
                to_owner(*target, i).start()
            band_in[core * PLANES + band, parts[i], :] = part[own, parts[i], :]

    def across_hi(k, i):
        mine = hi_in.at[hi, parts[i]]
        return send(mine, mine, sems.at[1, 0, i], sems.at[1, 1, i], to_hi[k])

    for i in range(2):
        @pl.when(has_plane)
        def _():
            bytes_of(band_in, 11, 0, i).wait_recv()

        @pl.when(jnp.logical_not(has_plane))
        def _():
            bytes_of(band_in, 12, 0, i).wait_recv()

        hi_in[hi, parts[i], :] = total_of(band_in, 12, i)
        for k in FAR_HI:
            across_hi(k, i).start()

    for c in range(CHUNKS):
        for r in range(3):
            for copy in halo(r, c):
                copy.wait_send()

    def across_z(k, i):
        mine = z_in.at[z, parts[i]]
        return send(mine, mine, sems.at[2, 0, i], sems.at[2, 1, i], to_z[k])

    for i in range(2):
        bytes_of(hi_in, 3, 1, i).wait_recv()
        z_in[z, parts[i], :] = total_of(hi_in, 4, i)
        for k in FAR_Z:
            across_z(k, i).start()

    def sent_planes(count):
        out = field.at[3, pl.ds(PLANES, count)]
        return send(out, out, cell_sems.at[0], cell_sems.at[1], left)

    @pl.when(jnp.logical_not(has_plane))
    def _():
        sent_planes(PLANES).wait_send()

    @pl.when(has_plane)
    def _():
        sent_planes(PLANES - 1).wait_send()
        for i in range(2):
            bytes_of(part, 15, 0, i).wait_send()

    def gather(where, i):
        mine = margin_ref.at[own, parts[i]]
        return send(mine, mine, sems.at[3, 0, i], sems.at[3, 1, i], where)

    for i in range(2):
        bytes_of(hi_in, 3, 1, i).wait_send()
        bytes_of(z_in, 7, 2, i).wait_recv()
        margin_ref[own, parts[i], :] = total_of(z_in, 8, i) * F32(1.0 / CELLS)
        for k, flip, where in to_sixteen:
            @pl.when(bands[k] < PLANES)
            def _():
                gather(where, i).start()

    def to_rows(half, k):
        target = half * 4 + lax.rem(band + k, 4)
        return send(made.at[rows_of(target)], out_ref.at[band],
                    row_sems.at[0, half * 4 + k], row_sems.at[1, band], (target, dom))

    def from_plane(p):
        return send(made.at[rows_of(0)], out_ref.at[p],
                    row_sems.at[0, 0], row_sems.at[1, p], (p, dom))

    lane = lax.broadcasted_iota(jnp.int32, (HALF, HALF), 1)
    row = lax.broadcasted_iota(jnp.int32, (HALF, HALF), 0)

    def block(i):
        return jnp.concatenate([margin_ref[q, 8 * i:8 * i + 8, :] for q in range(16)], axis=0)

    def factor_of(at):
        done = eliminate([work[at, 8 * g:8 * g + 8, :] for g in range(HALF // 8)], HALF)
        for g in range(HALF // 8):
            work[at, 8 * g:8 * g + 8, :] = done[g]
        return jnp.where(row >= lane, work[at], 0.0)

    def hand_out(half):
        for k in range(4):
            if k == 0:
                @pl.when(lax.div(band, 4) != half)
                def _():
                    to_rows(half, k).start()

                @pl.when(lax.div(band, 4) == half)
                def _():
                    out_ref[band] = made[rows_of(band), :]
            else:
                to_rows(half, k).start()

    @pl.when(jnp.logical_not(has_plane))
    def _():
        for i in range(2):
            bytes_of(z_in, 7, 2, i).wait_send()
            bytes_of(margin_ref, 12, 3, i).wait_send()

    @pl.when(has_plane)
    def _():
        bytes_of(margin_ref, 15, 3, 0).wait_recv()
        work[0] = block(0)
        first = factor_of(0)
        bytes_of(margin_ref, 15, 3, 1).wait_recv()
        below = product(block(1), first, ((1,), (1,)))
        work[1] = block(2) - product(below, below, ((1,), (1,)))
        made[:HALF, :] = product(first, cells_ref[:HALF, :])
        hand_out(0)
        for i in range(2):
            bytes_of(z_in, 7, 2, i).wait_send()
            bytes_of(margin_ref, 11, 3, i).wait_send()
        made[HALF:, :] = cells_ref[HALF:, :] - product(below, made[:HALF, :])
        second = factor_of(1)
        made[HALF:, :] = product(second, made[HALF:, :])
        hand_out(1)

    for p in range(PLANES):
        @pl.when(band != p)
        def _():
            from_plane(p).wait_recv()

    @pl.when(has_plane)
    def _():
        for half in range(2):
            for k in range(4):
                if k == 0:
                    @pl.when(lax.div(band, 4) != half)
                    def _():
                        to_rows(half, k).wait_send()
                else:
                    to_rows(half, k).wait_send()


def on_device(orbitals, potential):
    dma = pltpu.SemaphoreType.DMA
    piece = (24, 128)
    in_vmem = pl.BlockSpec(memory_space=pltpu.VMEM)
    planes = pl.pallas_call(
        whole_kernel,
        out_shape=pltpu.VMEM((PLANES, ORB, WIDTH), F32),
        in_specs=[pl.BlockSpec(memory_space=pltpu.HBM)] * 3,
        out_specs=in_vmem,
        scratch_shapes=[
            pltpu.VMEM((PLANES, WIDTH), F32),
            pltpu.VMEM((WIDTH, WIDTH), F32),
            pltpu.VMEM((BANDS, WIDTH), F32),
            pltpu.VMEM((16,) + piece, F32),
            pltpu.VMEM((BANDS, WIDTH), F32),
            pltpu.VMEM((2, HALF, HALF), F32),
            pltpu.VMEM((4, 3 * PLANES, ORB, WIDTH), F32),
            pltpu.VMEM((CHUNKS, PLANES, CORB, WIDTH), F32),
            pltpu.VMEM((16,) + piece, F32),
            pltpu.VMEM((2 * PLANES,) + piece, F32),
            pltpu.VMEM((4,) + piece, F32),
            pltpu.VMEM((8,) + piece, F32),
            dma((3, CHUNKS, 2)),
            dma((3, CHUNKS, 2)),
            dma((2,)),
            dma((3,)),
            dma((4, 2, 2)),
            dma((2, 8)),
        ],
        compiler_params=pltpu.CompilerParams(
            collective_id=0, has_side_effects=True, vmem_limit_bytes=54 * 1024 * 1024
        ),
        name="filter_orthonormalize",
    )(jnp.transpose(orbitals, (1, 0, 2)), potential, jnp.asarray(plane_matrix()))
    return jnp.transpose(planes, (1, 0, 2))


def solution(mesh):
    placed = (P("band", "dom", None), P("dom", None))
    return jax.shard_map(
        on_device, mesh=mesh, in_specs=placed, out_specs=P("band", "dom", None), check_vma=False
    )
```

time: 492 us -> 68.9 us (0.14)
  blocking collectives: 305 us -> 0 us
  Pallas kernels: 0 us -> 68.1 us
  other arithmetic: 61.8 us -> 0 us
  waiting for transfers between devices: 50 us -> 0 us
  starting transfers between devices: 35.2 us -> 0 us
  local copies, waits for them, and re-layouts: 17.5 us -> 0.68 us
  between operations: 15.8 us -> 0.01 us
  matrix products: 6.53 us -> 0 us
    psum x1 -> x0, blocking collectives: 276 us -> none  [on_device(): summed = lax.psum(rows, 'dom')]
    pallas_call x0 -> x1, Pallas kernels: none -> 68.1 us  [on_device(): pl.pallas_call(whole_kernel, out_shape=pltpu.VMEM((PLANES, ORB, WIDTH), F...]
    another operation x10 -> x0, other arithmetic: 54.3 us -> none  [the longest x7 34.6 us: inverse_factor(): factor = jnp.linalg.cholesky(margin)]
    all_gather x1 -> x0, waiting for transfers between devices: 45.6 us -> none  [on_device(): whole = lax.all_gather(filtered, 'band', axis=0, tiled=True)]
    ppermute x6 -> x0, starting transfers between devices: 35.2 us -> none  [the longest x3 29.3 us: with_halo(): lax.ppermute(head, axis, [((i + 1) % count, i) for i in range(count)])]
    all_gather x1 -> x0, blocking collectives: 28.4 us -> none  [on_device(): margin = lax.all_gather(summed, 'band', axis=0, tiled=True) / cells]
    slice x108 -> x0, local copies, waits for them, and re-layouts: 12.8 us -> none  [the longest x36 4.62 us: hamiltonian(): jnp.roll(field, step, 2)]
    sub x2 -> x0, other arithmetic: 5.41 us -> none  [the longest x1 3.04 us: on_device(): filtered = 2.0 * scaled(second, potential) - first]
  transfers between devices with their start and end apart: 7 -> 0, of which waited for: 4 -> 0; matrix products, arithmetic and copies ran while one was open for 2% -> 0% of each run, Pallas kernels for 0% -> 0%
where the time goes in v1:
time: 68.9 us; the launch traced here: 68.8 us
  Pallas kernels  68.1 us (99%)
    pallas_call x1, Pallas kernels, on_device(): pl.pallas_call(whole_kernel, out_shape=pltpu.VMEM((PLANES, ORB, WIDTH), F...  68.1 us

profile of v1, /device:TPU:8, one launch (start us, length us, event | category | flops | bytes accessed | tf_op | source)
XLA Modules:
  0.0 68.8 jit_solution(13851687940215974043)
XLA Ops:
  0.0 68.1 %filter_orthonormalize.1 = f32[6,32,256]{2,1,0:T(8,128)S(1)} custom-call(f32[6,32,256]{2,1,0:T(8,128)} %bitcast.3, f32[6,256]{1,0:T(8,128)} %pot_hbm.1, f32[256,256]{1,0:T(8,128)} %constant.2.clone.mat_hbm), custom_call_target="tpu_custom_call" | custom-call | tf_op jit(solution)/shard_map/filter_orthonormalize/pallas_call | solution.py:436
  68.1 0.7 copy.5

commit v2 on v1

--- a/solution.py
+++ b/solution.py
@@ -76,7 +76,7 @@
     return copy
 
 
-def eliminate(groups, size):
+def eliminate(groups, size, after_block=None):
     lane = lax.broadcasted_iota(jnp.int32, (8, size), 1)
     sublane = lax.broadcasted_iota(jnp.int32, (8, size), 0)
     groups = list(groups)
@@ -153,6 +153,8 @@
                 for q in span:
                     new = jnp.where(sublane == off + q, pivot_rows[q], new)
             groups[g] = new
+        if after_block is not None and following % ORB == 0:
+            after_block(following // ORB - 1, groups)
     return groups
 
 
@@ -160,7 +162,7 @@
     return pl.ds(pl.multiple_of(b * ORB, ORB), ORB)
 
 
-def whole_kernel(x_ref, pot_hbm, mat_hbm, out_ref, pot_ref, mat_ref, cells_ref, margin_ref, made, work,
+def whole_kernel(x_ref, pot_hbm, mat_hbm, out_ref, pot_ref, mat_ref, cells_ref, margin_ref, made, work, below_ref,
                  field, local, part, band_in, hi_in, z_in,
                  halo_send, halo_recv, cell_sems, load_sems, sems, row_sems):
     band = lax.axis_index("band")
@@ -189,7 +191,8 @@
         for k in FAR_BAND + (0,) for flip in range(2) if k + flip > 0
     ]
     own = core * 8 + band
-    greet([left, right] + [where for _, _, where in to_sixteen] + to_hi[1:] + to_z[1:])
+    greet([to_z[k] for k in FAR_Z] + [to_hi[k] for k in FAR_HI] + [left, right]
+          + [where for _, _, where in to_sixteen])
 
     def chunk(c):
         return pl.ds(c * CORB, CORB)
@@ -354,10 +357,9 @@
             def _():
                 gather(where, i).start()
 
-    def to_rows(half, k):
-        target = half * 4 + lax.rem(band + k, 4)
-        return send(made.at[rows_of(target)], out_ref.at[band],
-                    row_sems.at[0, half * 4 + k], row_sems.at[1, band], (target, dom))
+    def to_rows(t):
+        return send(made.at[pl.ds(t * ORB, ORB)], out_ref.at[band],
+                    row_sems.at[0, t], row_sems.at[1, band], (t, dom))
 
     def from_plane(p):
         return send(made.at[rows_of(0)], out_ref.at[p],
@@ -369,24 +371,38 @@
     def block(i):
         return jnp.concatenate([margin_ref[q, 8 * i:8 * i + 8, :] for q in range(16)], axis=0)
 
-    def factor_of(at):
-        done = eliminate([work[at, 8 * g:8 * g + 8, :] for g in range(HALF // 8)], HALF)
-        for g in range(HALF // 8):
-            work[at, 8 * g:8 * g + 8, :] = done[g]
-        return jnp.where(row >= lane, work[at], 0.0)
-
-    def hand_out(half):
-        for k in range(4):
-            if k == 0:
-                @pl.when(lax.div(band, 4) != half)
-                def _():
-                    to_rows(half, k).start()
-
-                @pl.when(lax.div(band, 4) == half)
-                def _():
-                    out_ref[band] = made[rows_of(band), :]
-            else:
-                to_rows(half, k).start()
+    def groups_of(at):
+        return [work[at, 8 * g:8 * g + 8, :] for g in range(HALF // 8)]
+
+    def hand_out(t):
+        @pl.when(band != t)
+        def _():
+            to_rows(t).start()
+
+        @pl.when(band == t)
+        def _():
+            out_ref[t] = made[t * ORB:(t + 1) * ORB, :]
+
+    def multiply(groups, begin, end):
+        rows = jnp.concatenate(groups[begin // 8:end // 8], axis=0)
+        rows = jnp.where(row[begin:end] >= lane[begin:end], rows, 0.0)
+        made[HALF + begin:HALF + end, :] = product(rows, cells_ref[HALF:, :])
+
+    def after_block(n, groups):
+        if n == 0:
+            for t in range(4):
+                hand_out(t)
+            cells_ref[HALF:, :] = cells_ref[HALF:, :] - product(below_ref[...], made[:HALF, :])
+        elif n == 1:
+            multiply(groups, 0, 2 * ORB)
+        elif n == 2:
+            hand_out(4)
+            hand_out(5)
+            multiply(groups, 2 * ORB, 3 * ORB)
+        else:
+            hand_out(6)
+            multiply(groups, 3 * ORB, 4 * ORB)
+            hand_out(7)
 
     @pl.when(jnp.logical_not(has_plane))
     def _():
@@ -398,19 +414,17 @@
     def _():
         bytes_of(margin_ref, 15, 3, 0).wait_recv()
         work[0] = block(0)
-        first = factor_of(0)
+        first = jnp.concatenate(eliminate(groups_of(0), HALF), axis=0)
+        first = jnp.where(row >= lane, first, 0.0)
         bytes_of(margin_ref, 15, 3, 1).wait_recv()
         below = product(block(1), first, ((1,), (1,)))
+        below_ref[...] = below
         work[1] = block(2) - product(below, below, ((1,), (1,)))
         made[:HALF, :] = product(first, cells_ref[:HALF, :])
-        hand_out(0)
+        eliminate(groups_of(1), HALF, after_block)
         for i in range(2):
             bytes_of(z_in, 7, 2, i).wait_send()
             bytes_of(margin_ref, 11, 3, i).wait_send()
-        made[HALF:, :] = cells_ref[HALF:, :] - product(below, made[:HALF, :])
-        second = factor_of(1)
-        made[HALF:, :] = product(second, made[HALF:, :])
-        hand_out(1)
 
     for p in range(PLANES):
         @pl.when(band != p)
@@ -419,14 +433,10 @@
 
     @pl.when(has_plane)
     def _():
-        for half in range(2):
-            for k in range(4):
-                if k == 0:
-                    @pl.when(lax.div(band, 4) != half)
-                    def _():
-                        to_rows(half, k).wait_send()
-                else:
-                    to_rows(half, k).wait_send()
+        for t in range(8):
+            @pl.when(band != t)
+            def _():
+                to_rows(t).wait_send()
 
 
 def on_device(orbitals, potential):
@@ -445,6 +455,7 @@
             pltpu.VMEM((16,) + piece, F32),
             pltpu.VMEM((BANDS, WIDTH), F32),
             pltpu.VMEM((2, HALF, HALF), F32),
+            pltpu.VMEM((HALF, HALF), F32),
             pltpu.VMEM((4, 3 * PLANES, ORB, WIDTH), F32),
             pltpu.VMEM((CHUNKS, PLANES, CORB, WIDTH), F32),
             pltpu.VMEM((16,) + piece, F32),

time: 68.9 us -> 67.2 us (0.975)
  the two profiles are of different devices: /device:TPU:8 before, /device:TPU:14 now
where the time goes in v2:
time: 67.2 us; the launch traced here: 67.1 us
  Pallas kernels  66.4 us (99%)
  local copies, waits for them, and re-layouts  0.68 us (1%)
    pallas_call x1, Pallas kernels, on_device(): pl.pallas_call(whole_kernel, out_shape=pltpu.VMEM((PLANES, ORB, WIDTH), F...  66.4 us

profile of v2, /device:TPU:14, one launch (start us, length us, event | category | flops | bytes accessed | tf_op | source)
XLA Modules:
  0.0 67.1 jit_solution(6221806381628675105)
XLA Ops:
  0.0 66.4 %filter_orthonormalize.1 = f32[6,32,256]{2,1,0:T(8,128)S(1)} custom-call(f32[6,32,256]{2,1,0:T(8,128)} %bitcast.3, f32[6,256]{1,0:T(8,128)} %pot_hbm.1, f32[256,256]{1,0:T(8,128)} %constant.2.clone.mat_hbm), custom_call_target="tpu_custom_call" | custom-call | tf_op jit(solution)/shard_map/filter_orthonormalize/pallas_call | solution.py:446
  66.4 0.7 %copy.5 = f32[32,6,256]{2,0,1:T(8,128)} copy(f32[32,6,256]{2,0,1:T(8,128)S(1)} %bitcast.2) | data formatting | bytes 393216

commit v3 on v2

--- a/solution.py
+++ b/solution.py
@@ -76,7 +76,7 @@
     return copy
 
 
-def eliminate(groups, size, after_block=None):
+def eliminate(groups, size, after_rows=None):
     lane = lax.broadcasted_iota(jnp.int32, (8, size), 1)
     sublane = lax.broadcasted_iota(jnp.int32, (8, size), 0)
     groups = list(groups)
@@ -153,8 +153,8 @@
                 for q in span:
                     new = jnp.where(sublane == off + q, pivot_rows[q], new)
             groups[g] = new
-        if after_block is not None and following % ORB == 0:
-            after_block(following // ORB - 1, groups)
+        if after_rows is not None:
+            after_rows(following, groups)
     return groups
 
 
@@ -315,34 +315,37 @@
         for k in FAR_HI:
             across_hi(k, i).start()
 
-    for c in range(CHUNKS):
-        for r in range(3):
-            for copy in halo(r, c):
-                copy.wait_send()
-
     def across_z(k, i):
         mine = z_in.at[z, parts[i]]
         return send(mine, mine, sems.at[2, 0, i], sems.at[2, 1, i], to_z[k])
+
+    def sent_planes(count):
+        out = field.at[3, pl.ds(PLANES, count)]
+        return send(out, out, cell_sems.at[0], cell_sems.at[1], left)
+
+    def filter_sent():
+        for c in range(CHUNKS):
+            for r in range(3):
+                for copy in halo(r, c):
+                    copy.wait_send()
+
+        @pl.when(jnp.logical_not(has_plane))
+        def _():
+            sent_planes(PLANES).wait_send()
+
+        @pl.when(has_plane)
+        def _():
+            sent_planes(PLANES - 1).wait_send()
+            for i in range(2):
+                bytes_of(part, 15, 0, i).wait_send()
 
     for i in range(2):
         bytes_of(hi_in, 3, 1, i).wait_recv()
         z_in[z, parts[i], :] = total_of(hi_in, 4, i)
         for k in FAR_Z:
             across_z(k, i).start()
-
-    def sent_planes(count):
-        out = field.at[3, pl.ds(PLANES, count)]
-        return send(out, out, cell_sems.at[0], cell_sems.at[1], left)
-
-    @pl.when(jnp.logical_not(has_plane))
-    def _():
-        sent_planes(PLANES).wait_send()
-
-    @pl.when(has_plane)
-    def _():
-        sent_planes(PLANES - 1).wait_send()
-        for i in range(2):
-            bytes_of(part, 15, 0, i).wait_send()
+        if i == 0:
+            filter_sent()
 
     def gather(where, i):
         mine = margin_ref.at[own, parts[i]]
@@ -357,8 +360,8 @@
             def _():
                 gather(where, i).start()
 
-    def to_rows(t):
-        return send(made.at[pl.ds(t * ORB, ORB)], out_ref.at[band],
+    def to_rows(t, begin=0, count=ORB):
+        return send(made.at[pl.ds(t * ORB + begin, count)], out_ref.at[band, pl.ds(begin, count)],
                     row_sems.at[0, t], row_sems.at[1, band], (t, dom))
 
     def from_plane(p):
@@ -374,35 +377,38 @@
     def groups_of(at):
         return [work[at, 8 * g:8 * g + 8, :] for g in range(HALF // 8)]
 
-    def hand_out(t):
+    def hand_out(t, begin=0, count=ORB):
         @pl.when(band != t)
         def _():
-            to_rows(t).start()
+            to_rows(t, begin, count).start()
 
         @pl.when(band == t)
         def _():
-            out_ref[t] = made[t * ORB:(t + 1) * ORB, :]
+            out_ref[t, begin:begin + count, :] = made[t * ORB + begin:t * ORB + begin + count, :]
 
     def multiply(groups, begin, end):
         rows = jnp.concatenate(groups[begin // 8:end // 8], axis=0)
         rows = jnp.where(row[begin:end] >= lane[begin:end], rows, 0.0)
         made[HALF + begin:HALF + end, :] = product(rows, cells_ref[HALF:, :])
 
-    def after_block(n, groups):
-        if n == 0:
+    def after_rows(n, groups):
+        if n == 32:
             for t in range(4):
                 hand_out(t)
             cells_ref[HALF:, :] = cells_ref[HALF:, :] - product(below_ref[...], made[:HALF, :])
-        elif n == 1:
-            multiply(groups, 0, 2 * ORB)
-        elif n == 2:
+        elif n == 64:
+            multiply(groups, 0, 64)
+        elif n == 96:
             hand_out(4)
             hand_out(5)
-            multiply(groups, 2 * ORB, 3 * ORB)
-        else:
+            multiply(groups, 64, 96)
+        elif n == 112:
             hand_out(6)
-            multiply(groups, 3 * ORB, 4 * ORB)
-            hand_out(7)
+            multiply(groups, 96, 112)
+        elif n == 128:
+            hand_out(7, 0, 16)
+            multiply(groups, 112, 128)
+            hand_out(7, 16, 16)
 
     @pl.when(jnp.logical_not(has_plane))
     def _():
@@ -421,7 +427,7 @@
         below_ref[...] = below
         work[1] = block(2) - product(below, below, ((1,), (1,)))
         made[:HALF, :] = product(first, cells_ref[:HALF, :])
-        eliminate(groups_of(1), HALF, after_block)
+        eliminate(groups_of(1), HALF, after_rows)
         for i in range(2):
             bytes_of(z_in, 7, 2, i).wait_send()
             bytes_of(margin_ref, 11, 3, i).wait_send()

time: 67.2 us -> 67.1 us (level)
  no operation moved by 1% of the time
where the time goes in v3:
time: 67.1 us; the launch traced here: 67 us
  Pallas kernels  66.3 us (99%)
  local copies, waits for them, and re-layouts  0.68 us (1%)
    pallas_call x1, Pallas kernels, on_device(): pl.pallas_call(whole_kernel, out_shape=pltpu.VMEM((PLANES, ORB, WIDTH), F...  66.3 us

profile of v3, /device:TPU:14, one launch (start us, length us, event | category | flops | bytes accessed | tf_op | source)
XLA Modules:
  0.0 67.0 jit_solution(16293219543834504206)
XLA Ops:
  0.0 66.3 %filter_orthonormalize.1 = f32[6,32,256]{2,1,0:T(8,128)S(1)} custom-call(f32[6,32,256]{2,1,0:T(8,128)} %bitcast.3, f32[6,256]{1,0:T(8,128)} %pot_hbm.1, f32[256,256]{1,0:T(8,128)} %constant.2.clone.mat_hbm), custom_call_target="tpu_custom_call" | custom-call | tf_op jit(solution)/shard_map/filter_orthonormalize/pallas_call | solution.py:452
  66.3 0.7 %copy.5 = f32[32,6,256]{2,0,1:T(8,128)} copy(f32[32,6,256]{2,0,1:T(8,128)S(1)} %bitcast.2) | data formatting | bytes 393216

commit v4 on v3

--- a/solution.py
+++ b/solution.py
@@ -197,16 +197,14 @@
     def chunk(c):
         return pl.ds(c * CORB, CORB)
 
-    def halo(r, c):
-        if r == 0:
-            own = x_ref.at[:, chunk(c)]
-        else:
-            own = field.at[r, pl.ds(PLANES, PLANES), chunk(c)]
+    def halo(r, c, h):
+        side = pl.ds(h * 128, 128)
+        own = field.at[r, pl.ds(PLANES, PLANES), chunk(c), side]
         return (
-            send(own, field.at[r, pl.ds(2 * PLANES, PLANES), chunk(c)],
-                 halo_send.at[r, c, 0], halo_recv.at[r, c, 0], left),
-            send(own, field.at[r, pl.ds(0, PLANES), chunk(c)],
-                 halo_send.at[r, c, 1], halo_recv.at[r, c, 1], right),
+            send(own, field.at[r, pl.ds(2 * PLANES, PLANES), chunk(c), side],
+                 halo_send.at[r, c, h, 0], halo_recv.at[r, c, h, 0], left),
+            send(own, field.at[r, pl.ds(0, PLANES), chunk(c), side],
+                 halo_send.at[r, c, h, 1], halo_recv.at[r, c, h, 1], right),
         )
 
     def in_plane(r, c):
@@ -228,30 +226,34 @@
         others = cells_ref.at[pl.ds(0, BANDS - ORB)]
         return send(others, others, cell_sems.at[0], cell_sems.at[1], to_band[1])
 
-    for c in range(CHUNKS):
-        for copy in halo(0, c):
-            copy.start()
     for load in loads:
         load.wait()
+    for c in range(CHUNKS):
+        for h in range(2):
+            for copy in halo(0, c, h):
+                copy.start()
     for c in range(CHUNKS):
         in_plane(0, c)
     for r in range(3):
         for c in range(CHUNKS):
             rows = slice(c * CORB, (c + 1) * CORB)
-            for copy in halo(r, c):
-                copy.wait_recv()
-            for p in range(PLANES):
-                total = local[c, p]
-                for step in range(1, 7):
-                    total = total + along_z[step] * (
-                        field[r, PLANES + p - step, rows, :] + field[r, PLANES + p + step, rows, :]
-                    )
-                if r > 0:
-                    total = 2.0 * total - field[r - 1, PLANES + p, rows, :]
-                field[r + 1, PLANES + p, rows, :] = total
+            for h in range(2):
+                side = slice(h * 128, (h + 1) * 128)
+                for copy in halo(r, c, h):
+                    copy.wait_recv()
+                for p in range(PLANES):
+                    total = local[c, p, :, side]
+                    for step in range(1, 7):
+                        total = total + along_z[step] * (
+                            field[r, PLANES + p - step, rows, side] + field[r, PLANES + p + step, rows, side]
+                        )
+                    if r > 0:
+                        total = 2.0 * total - field[r - 1, PLANES + p, rows, side]
+                    field[r + 1, PLANES + p, rows, side] = total
+                if r < 2:
+                    for copy in halo(r + 1, c, h):
+                        copy.start()
             if r < 2:
-                for copy in halo(r + 1, c):
-                    copy.start()
                 in_plane(r + 1, c)
             else:
                 for k in FAR_BAND:
@@ -326,8 +328,9 @@
     def filter_sent():
         for c in range(CHUNKS):
             for r in range(3):
-                for copy in halo(r, c):
-                    copy.wait_send()
+                for h in range(2):
+                    for copy in halo(r, c, h):
+                        copy.wait_send()
 
         @pl.when(jnp.logical_not(has_plane))
         def _():
@@ -468,8 +471,8 @@
             pltpu.VMEM((2 * PLANES,) + piece, F32),
             pltpu.VMEM((4,) + piece, F32),
             pltpu.VMEM((8,) + piece, F32),
-            dma((3, CHUNKS, 2)),
-            dma((3, CHUNKS, 2)),
+            dma((3, CHUNKS, 2, 2)),
+            dma((3, CHUNKS, 2, 2)),
             dma((2,)),
             dma((3,)),
             dma((4, 2, 2)),

time: 67.1 us -> 67.3 us (level)
  no operation moved by 1% of the time
where the time goes in v4:
time: 67.3 us; the launch traced here: 67.2 us
  Pallas kernels  66.5 us (99%)
  local copies, waits for them, and re-layouts  0.68 us (1%)
    pallas_call x1, Pallas kernels, on_device(): pl.pallas_call(whole_kernel, out_shape=pltpu.VMEM((PLANES, ORB, WIDTH), F...  66.5 us

profile of v4, /device:TPU:14, one launch (start us, length us, event | category | flops | bytes accessed | tf_op | source)
XLA Modules:
  0.0 67.2 jit_solution(12133842167092111774)
XLA Ops:
  0.0 66.5 %filter_orthonormalize.1 = f32[6,32,256]{2,1,0:T(8,128)S(1)} custom-call(f32[6,32,256]{2,1,0:T(8,128)} %bitcast.3, f32[6,256]{1,0:T(8,128)} %pot_hbm.1, f32[256,256]{1,0:T(8,128)} %constant.2.clone.mat_hbm), custom_call_target="tpu_custom_call" | custom-call | tf_op jit(solution)/shard_map/filter_orthonormalize/pallas_call | solution.py:455
  66.5 0.7 %copy.5 = f32[32,6,256]{2,0,1:T(8,128)} copy(f32[32,6,256]{2,0,1:T(8,128)S(1)} %bitcast.2) | data formatting | bytes 393216

commit v5 on v3

--- a/solution.py
+++ b/solution.py
@@ -174,7 +174,6 @@
     left = (band, lax.rem(dom + count - 1, count))
     right = (band, lax.rem(dom + 1, count))
     bands = [lax.rem(band + k, 8) for k in range(8)]
-    senders = [lax.rem(band + 8 - k, 8) for k in range(8)]
     to_band = [(bands[k], dom) for k in range(8)]
     to_hi = [(band, z * 8 + lax.rem(hi + k, 4) * 2 + core) for k in range(4)]
     to_z = [(band, lax.rem(z + k, 8) * 8 + hi * 2 + core) for k in range(8)]
@@ -190,7 +189,6 @@
         (k, flip, (bands[k], dom + flip * (1 - 2 * core)))
         for k in FAR_BAND + (0,) for flip in range(2) if k + flip > 0
     ]
-    own = core * 8 + band
     greet([to_z[k] for k in FAR_Z] + [to_hi[k] for k in FAR_HI] + [left, right]
           + [where for _, _, where in to_sixteen])
 
@@ -263,10 +261,7 @@
                 def _():
                     cells_ref[rows_in(c), :] = field[3, PLANES + band, rows, :]
 
-    def sixteenth(k, flip):
-        return (core + flip * (1 - 2 * core)) * 8 + bands[k]
-
-    parts = (pl.ds(0, 8), pl.ds(8, 16))
+    parts = (pl.ds(0, 16), pl.ds(16, 32))
 
     def total_of(ref, count, i):
         total = ref[0, parts[i], :]
@@ -278,9 +273,9 @@
         some = ref.at[pl.ds(0, count), parts[i]]
         return send(some, some, sems.at[stage, 0, i], sems.at[stage, 1, i], left)
 
-    def to_owner(k, flip, where, i):
-        return send(part.at[sixteenth(k, flip), parts[i]], band_in.at[core * PLANES + band, parts[i]],
-                    sems.at[0, 0, i], sems.at[0, 1, i], where)
+    def to_owner(k, i):
+        return send(part.at[bands[k], parts[i]], band_in.at[core * PLANES + band, parts[i]],
+                    sems.at[0, 0, i], sems.at[0, 1, i], (bands[k], dom - core + i))
 
     @pl.when(has_plane)
     def _():
@@ -291,29 +286,23 @@
             else:
                 both = product(cells_ref[HALF:, :], cells_ref[...], ((1,), (1,)))
                 blocks = (both[:, :HALF], both[:, HALF:])
-            for q in range(16):
+            for q in range(8):
                 for n, piece in enumerate(blocks):
-                    part[q, 8 * (i + n):8 * (i + n) + 8, :] = piece[8 * q:8 * q + 8, :]
-            for target in to_sixteen:
-                to_owner(*target, i).start()
-            band_in[core * PLANES + band, parts[i], :] = part[own, parts[i], :]
+                    part[q, 16 * (i + n):16 * (i + n) + 16, :] = piece[16 * q:16 * q + 16, :]
+            for k in FAR_BAND:
+                to_owner(k, i).start()
+
+            @pl.when(core != i)
+            def _():
+                to_owner(0, i).start()
+
+            @pl.when(core == i)
+            def _():
+                band_in[core * PLANES + band, parts[i], :] = part[band, parts[i], :]
 
     def across_hi(k, i):
         mine = hi_in.at[hi, parts[i]]
         return send(mine, mine, sems.at[1, 0, i], sems.at[1, 1, i], to_hi[k])
-
-    for i in range(2):
-        @pl.when(has_plane)
-        def _():
-            bytes_of(band_in, 11, 0, i).wait_recv()
-
-        @pl.when(jnp.logical_not(has_plane))
-        def _():
-            bytes_of(band_in, 12, 0, i).wait_recv()
-
-        hi_in[hi, parts[i], :] = total_of(band_in, 12, i)
-        for k in FAR_HI:
-            across_hi(k, i).start()
 
     def across_z(k, i):
         mine = z_in.at[z, parts[i]]
@@ -337,28 +326,61 @@
         def _():
             sent_planes(PLANES - 1).wait_send()
             for i in range(2):
-                bytes_of(part, 15, 0, i).wait_send()
-
-    for i in range(2):
+                @pl.when(core == i)
+                def _():
+                    bytes_of(part, 7, 0, i).wait_send()
+
+                @pl.when(core != i)
+                def _():
+                    bytes_of(part, 8, 0, i).wait_send()
+
+    def gather(where, i):
+        mine = margin_ref.at[band, parts[i]]
+        return send(mine, mine, sems.at[3, 0, i], sems.at[3, 1, i], where)
+
+    def sum_part(i):
+        @pl.when(has_plane)
+        def _():
+            bytes_of(band_in, 11, 0, i).wait_recv()
+
+        @pl.when(jnp.logical_not(has_plane))
+        def _():
+            bytes_of(band_in, 12, 0, i).wait_recv()
+
+        hi_in[hi, parts[i], :] = total_of(band_in, 12, i)
+        for k in FAR_HI:
+            across_hi(k, i).start()
+        filter_sent()
         bytes_of(hi_in, 3, 1, i).wait_recv()
         z_in[z, parts[i], :] = total_of(hi_in, 4, i)
         for k in FAR_Z:
             across_z(k, i).start()
-        if i == 0:
-            filter_sent()
-
-    def gather(where, i):
-        mine = margin_ref.at[own, parts[i]]
-        return send(mine, mine, sems.at[3, 0, i], sems.at[3, 1, i], where)
-
-    for i in range(2):
         bytes_of(hi_in, 3, 1, i).wait_send()
         bytes_of(z_in, 7, 2, i).wait_recv()
-        margin_ref[own, parts[i], :] = total_of(z_in, 8, i) * F32(1.0 / CELLS)
+        margin_ref[band, parts[i], :] = total_of(z_in, 8, i) * F32(1.0 / CELLS)
         for k, flip, where in to_sixteen:
             @pl.when(bands[k] < PLANES)
             def _():
                 gather(where, i).start()
+        bytes_of(z_in, 7, 2, i).wait_send()
+
+        @pl.when(jnp.logical_not(has_plane))
+        def _():
+            bytes_of(margin_ref, 12, 3, i).wait_send()
+
+    for i in range(2):
+        @pl.when(core == i)
+        def _():
+            sum_part(i)
+
+    def await_part(i):
+        @pl.when(core == i)
+        def _():
+            bytes_of(margin_ref, 7, 3, i).wait_recv()
+
+        @pl.when(core != i)
+        def _():
+            bytes_of(margin_ref, 8, 3, i).wait_recv()
 
     def to_rows(t, begin=0, count=ORB):
         return send(made.at[pl.ds(t * ORB + begin, count)], out_ref.at[band, pl.ds(begin, count)],
@@ -372,7 +394,7 @@
     row = lax.broadcasted_iota(jnp.int32, (HALF, HALF), 0)
 
     def block(i):
-        return jnp.concatenate([margin_ref[q, 8 * i:8 * i + 8, :] for q in range(16)], axis=0)
+        return jnp.concatenate([margin_ref[q, 16 * i:16 * i + 16, :] for q in range(8)], axis=0)
 
     def groups_of(at):
         return [work[at, 8 * g:8 * g + 8, :] for g in range(HALF // 8)]
@@ -410,27 +432,22 @@
             multiply(groups, 112, 128)
             hand_out(7, 16, 16)
 
-    @pl.when(jnp.logical_not(has_plane))
-    def _():
-        for i in range(2):
-            bytes_of(z_in, 7, 2, i).wait_send()
-            bytes_of(margin_ref, 12, 3, i).wait_send()
-
     @pl.when(has_plane)
     def _():
-        bytes_of(margin_ref, 15, 3, 0).wait_recv()
+        await_part(0)
         work[0] = block(0)
         first = jnp.concatenate(eliminate(groups_of(0), HALF), axis=0)
         first = jnp.where(row >= lane, first, 0.0)
-        bytes_of(margin_ref, 15, 3, 1).wait_recv()
+        await_part(1)
         below = product(block(1), first, ((1,), (1,)))
         below_ref[...] = below
         work[1] = block(2) - product(below, below, ((1,), (1,)))
         made[:HALF, :] = product(first, cells_ref[:HALF, :])
         eliminate(groups_of(1), HALF, after_rows)
         for i in range(2):
-            bytes_of(z_in, 7, 2, i).wait_send()
-            bytes_of(margin_ref, 11, 3, i).wait_send()
+            @pl.when(core == i)
+            def _():
+                bytes_of(margin_ref, 11, 3, i).wait_send()
 
     for p in range(PLANES):
         @pl.when(band != p)
@@ -447,7 +464,7 @@
 
 def on_device(orbitals, potential):
     dma = pltpu.SemaphoreType.DMA
-    piece = (24, 128)
+    piece = (48, 128)
     in_vmem = pl.BlockSpec(memory_space=pltpu.VMEM)
     planes = pl.pallas_call(
         whole_kernel,
@@ -458,13 +475,13 @@
             pltpu.VMEM((PLANES, WIDTH), F32),
             pltpu.VMEM((WIDTH, WIDTH), F32),
             pltpu.VMEM((BANDS, WIDTH), F32),
-            pltpu.VMEM((16,) + piece, F32),
+            pltpu.VMEM((2 * PLANES,) + piece, F32),
             pltpu.VMEM((BANDS, WIDTH), F32),
             pltpu.VMEM((2, HALF, HALF), F32),
             pltpu.VMEM((HALF, HALF), F32),
             pltpu.VMEM((4, 3 * PLANES, ORB, WIDTH), F32),
             pltpu.VMEM((CHUNKS, PLANES, CORB, WIDTH), F32),
-            pltpu.VMEM((16,) + piece, F32),
+            pltpu.VMEM((8,) + piece, F32),
             pltpu.VMEM((2 * PLANES,) + piece, F32),
             pltpu.VMEM((4,) + piece, F32),
             pltpu.VMEM((8,) + piece, F32),

time: 67.1 us -> 68.2 us (1.016)
  Pallas kernels: 66.3 us -> 67.4 us
    pallas_call x1, Pallas kernels: 66.3 us -> 67.4 us  [on_device(): pl.pallas_call(whole_kernel, out_shape=pltpu.VMEM((PLANES, ORB, WIDTH), F...]
where the time goes in v5:
time: 68.2 us; the launch traced here: 68.1 us
  Pallas kernels  67.4 us (99%)
    pallas_call x1, Pallas kernels, on_device(): pl.pallas_call(whole_kernel, out_shape=pltpu.VMEM((PLANES, ORB, WIDTH), F...  67.4 us

profile of v5, /device:TPU:14, one launch (start us, length us, event | category | flops | bytes accessed | tf_op | source)
XLA Modules:
  0.0 68.1 jit_solution(13304644924955406380)
XLA Ops:
  0.0 67.4 %filter_orthonormalize.1 = f32[6,32,256]{2,1,0:T(8,128)S(1)} custom-call(f32[6,32,256]{2,1,0:T(8,128)} %bitcast.3, f32[6,256]{1,0:T(8,128)} %pot_hbm.1, f32[256,256]{1,0:T(8,128)} %constant.2.clone.mat_hbm), custom_call_target="tpu_custom_call" | custom-call | tf_op jit(solution)/shard_map/filter_orthonormalize/pallas_call | solution.py:469
  67.4 0.7 copy.5

commit v6 on v3

--- a/solution.py
+++ b/solution.py
@@ -192,16 +192,13 @@
     ]
     own = core * 8 + band
     greet([to_z[k] for k in FAR_Z] + [to_hi[k] for k in FAR_HI] + [left, right]
-          + [where for _, _, where in to_sixteen])
+          + [where for k, _, where in to_sixteen if k > 0])
 
     def chunk(c):
         return pl.ds(c * CORB, CORB)
 
     def halo(r, c):
-        if r == 0:
-            own = x_ref.at[:, chunk(c)]
-        else:
-            own = field.at[r, pl.ds(PLANES, PLANES), chunk(c)]
+        own = field.at[r, pl.ds(PLANES, PLANES), chunk(c)]
         return (
             send(own, field.at[r, pl.ds(2 * PLANES, PLANES), chunk(c)],
                  halo_send.at[r, c, 0], halo_recv.at[r, c, 0], left),
@@ -228,11 +225,11 @@
         others = cells_ref.at[pl.ds(0, BANDS - ORB)]
         return send(others, others, cell_sems.at[0], cell_sems.at[1], to_band[1])
 
+    for load in loads:
+        load.wait()
     for c in range(CHUNKS):
         for copy in halo(0, c):
             copy.start()
-    for load in loads:
-        load.wait()
     for c in range(CHUNKS):
         in_plane(0, c)
     for r in range(3):
@@ -355,10 +352,12 @@
         bytes_of(hi_in, 3, 1, i).wait_send()
         bytes_of(z_in, 7, 2, i).wait_recv()
         margin_ref[own, parts[i], :] = total_of(z_in, 8, i) * F32(1.0 / CELLS)
-        for k, flip, where in to_sixteen:
+        for k in FAR_BAND + (0,):
             @pl.when(bands[k] < PLANES)
             def _():
-                gather(where, i).start()
+                for other, _, where in to_sixteen:
+                    if other == k:
+                        gather(where, i).start()
 
     def to_rows(t, begin=0, count=ORB):
         return send(made.at[pl.ds(t * ORB + begin, count)], out_ref.at[band, pl.ds(begin, count)],
@@ -405,10 +404,13 @@
         elif n == 112:
             hand_out(6)
             multiply(groups, 96, 112)
+        elif n == 120:
+            hand_out(7, 0, 16)
+            multiply(groups, 112, 120)
         elif n == 128:
-            hand_out(7, 0, 16)
-            multiply(groups, 112, 128)
-            hand_out(7, 16, 16)
+            hand_out(7, 16, 8)
+            multiply(groups, 120, 128)
+            hand_out(7, 24, 8)
 
     @pl.when(jnp.logical_not(has_plane))
     def _():

time: 67.1 us -> 66.9 us (level)
  no operation moved by 1% of the time
where the time goes in v6:
time: 66.9 us; the launch traced here: 66.8 us
  Pallas kernels  66.1 us (99%)
  local copies, waits for them, and re-layouts  0.68 us (1%)
    pallas_call x1, Pallas kernels, on_device(): pl.pallas_call(whole_kernel, out_shape=pltpu.VMEM((PLANES, ORB, WIDTH), F...  66.1 us

profile of v6, /device:TPU:14, one launch (start us, length us, event | category | flops | bytes accessed | tf_op | source)
XLA Modules:
  0.0 66.8 jit_solution(14349244673339033460)
XLA Ops:
  0.0 66.1 %filter_orthonormalize.1 = f32[6,32,256]{2,1,0:T(8,128)S(1)} custom-call(f32[6,32,256]{2,1,0:T(8,128)} %bitcast.3, f32[6,256]{1,0:T(8,128)} %pot_hbm.1, f32[256,256]{1,0:T(8,128)} %constant.2.clone.mat_hbm), custom_call_target="tpu_custom_call" | custom-call | tf_op jit(solution)/shard_map/filter_orthonormalize/pallas_call | solution.py:454
  66.1 0.7 %copy.5 = f32[32,6,256]{2,0,1:T(8,128)} copy(f32[32,6,256]{2,0,1:T(8,128)S(1)} %bitcast.2) | data formatting | bytes 393216
